TPU v7x, 32 devices: a whole 2x2x4 slice. The times are simulated.
32 devices in a mesh: task: 4 (over y, x), shard: 8 (over z, core).
Axes of the slice: x: 2, y: 2, z: 4, core: 2. Of those that a mesh axis runs over, the one named last changes fastest.
Arguments:
- tokens: bfloat16 [1024, 4096], P(('task', 'shard')), may hold values from -600 to 600
- gain: float32 [4096], replicated, may hold values from 0.5 to 1.5
- task_ids: int32 [1024], P(('task', 'shard')), may hold values from 0 to 7, as said below
- order: int32 [1024], P(('task', 'shard')), may hold values from 0 to 31, as said below
- w_gate: bfloat16 [8, 4096, 14336], P('task', None, 'shard'), may hold values from -0.09375 to 0.09375
- w_up: bfloat16 [8, 4096, 14336], P('task', None, 'shard'), may hold values from -0.09375 to 0.09375
- w_down: bfloat16 [8, 14336, 4096], P('task', 'shard'), may hold values from -0.046875 to 0.046875
Outputs:
- mixed: bfloat16 [1024, 4096], P(('task', 'shard'))
Inputs may be any that keep to these rules, and one draw needn't show every extreme that they name: `task_ids`: in each aligned block of 32 rows (the rows of one device) at most 8 rows name any one task; one task, the same for all blocks, is named by exactly 8 rows of every block. `order`: each aligned block of 32 entries is a permutation of 0 to 31.
All inputs are finite; a program needn't handle non-finite values.
Results may differ from a plain program's by a relative error of at most 0.015.
Values may be sent and summed in bfloat16 or wider, within the bound.
A program may use at most 192 MiB of HBM per device.

v0:
```python
import jax
import jax.numpy as jnp
from jax import lax
from jax.sharding import PartitionSpec as P

CAP = 8


epsilon = 1e-06


def expert_block(gathered_rows, w_gate, w_up, w_down):
    gate_value = jnp.einsum(
        "red,edf->ref", gathered_rows, w_gate, preferred_element_type=jnp.float32
    )
    up_value = jnp.einsum("red,edf->ref", gathered_rows, w_up, preferred_element_type=jnp.float32)
    hidden = (jax.nn.silu(gate_value) * up_value).astype(jnp.bfloat16)
    return jnp.einsum("ref,efd->red", hidden, w_down, preferred_element_type=jnp.float32)


def shards(tokens, gain, task_ids, order, w_gate, w_up, w_down):
    task_count = lax.axis_size("task")
    local_experts = w_gate.shape[0]
    expert_count = task_count * local_experts
    feature_count = tokens.shape[1]
    values = tokens.astype(jnp.float32)
    mean_square = jnp.mean(values * values, axis=-1, keepdims=True)
    normed = (values * lax.rsqrt(mean_square + epsilon) * gain).astype(jnp.bfloat16)
    onehot = (task_ids[:, None] == jnp.arange(expert_count, dtype=jnp.int32)[None, :]).astype(
        jnp.int32
    )
    position = jnp.sum(jnp.cumsum(onehot, axis=0) * onehot, axis=1) - 1
    slot_index = (
        task_ids // local_experts * CAP + position
    ) * local_experts + task_ids % local_experts
    slot_count = task_count * CAP * local_experts
    slot_range = jnp.arange(slot_count, dtype=jnp.int32)
    placing = (slot_index[:, None] == slot_range[None, :]).astype(jnp.bfloat16)
    outgoing = jnp.einsum("rs,rd->sd", placing, normed, preferred_element_type=jnp.float32).astype(
        jnp.bfloat16
    )
    outgoing = outgoing.reshape(task_count, CAP, local_experts, feature_count)
    arrived = lax.all_to_all(outgoing, "task", split_axis=0, concat_axis=0, tiled=True)
    local_rows = arrived.reshape(task_count * CAP, local_experts, feature_count)
    partial_terms = expert_block(
        lax.all_gather(local_rows, "shard", axis=0, tiled=True), w_gate, w_up, w_down
    )
    summed = lax.psum_scatter(
        partial_terms.astype(jnp.bfloat16), "shard", scatter_dimension=0, tiled=True
    )
    results = summed.reshape(task_count, CAP, local_experts, feature_count)
    returned = lax.all_to_all(results, "task", split_axis=0, concat_axis=0, tiled=True)
    returned = returned.reshape(slot_count, feature_count)
    wanted = jnp.take(slot_index, order)
    selecting = (wanted[:, None] == slot_range[None, :]).astype(jnp.bfloat16)
    return jnp.dot(selecting, returned, preferred_element_type=jnp.float32).astype(jnp.bfloat16)


def solution(mesh):
    placed = (
        P(("task", "shard"), None),
        P(),
        P(("task", "shard")),
        P(("task", "shard")),
        P("task", None, "shard"),
        P("task", None, "shard"),
        P("task", "shard", None),
    )
    return jax.shard_map(
        shards, mesh=mesh, in_specs=placed, out_specs=P(("task", "shard"), None), check_vma=False
    )
```

profile of v0, /device:TPU:0, one launch (start us, length us, event | category | flops | bytes accessed | tf_op | source)
XLA Modules:
  0.0 191.5 jit_solution(2983325939578157810)
XLA Ops:
  6.5 0.0 all-gather.2.cloned.1.call-start
  6.5 1.1 fusion.5
  7.7 0.7 fusion.11
  8.4 0.1 reduce_window_sum.11
  8.4 0.8 select_reduce_fusion
  9.3 0.7 fusion.14
  10.0 1.4 convolution_convert_fusion.1
  11.3 0.3 reshape.30
  11.7 13.5 %all_to_all.10 = bf16[4,8,2,4096]{3,2,1,0:T(2,128)(2,1)S(1)} all-to-all(bf16[4,8,2,4096]{3,2,1,0:T(2,128)(2,1)S(1)} %reshape.30), channel_id=1, replica_groups=mesh['task'=4,'shard'=8] {'task'}, dimensions={0} | all-to-all | bytes 1048576 | tf_op jit(solution)/shard_map/all_to_all | solution.py:43
  25.2 1.1 copy.12
  26.2 0.0 all-gather.2.cloned.1.call-update
  26.3 0.0 reduce-scatter.2.cloned.1.call-start
  26.3 47.0 %all-gather.2.cloned.1.call-done = bf16[256,2,4096]{2,0,1:T(8,128)(2,1)} async-done(((bf16[32,2,4096]{2,0,1:T(8,128)(2,1)}), bf16[256,2,4096]{2,0,1:T(8,128)(2,1)}) %all-gather.2.cloned.1.call-update) | async-done | bytes 4194320 | tf_op jit(solution)/shard_map/all_gather | solution.py:46
  73.3 16.8 %fusion.15 = f32[2,256,1792]{2,1,0:T(8,128)} fusion(bf16[256,2,4096]{2,0,1:T(8,128)(2,1)} %all-gather.2.cloned.1.call-done, bf16[2,4096,1792]{2,1,0:T(8,128)(2,1)} %param.11), kind=kOutput, calls=%fused_computation.37 | convolution fusion | flops 7516192768 | bytes 37224448 | tf_op jit(solution)/shard_map/red,edf->ref/dot_general | solution.py:13
  90.1 31.8 %fusion = bf16[256,2,4096]{2,0,1:T(8,128)(2,1)} fusion(bf16[2,1792,4096]{2,1,0:T(8,128)(2,1)} %param.13, f32[2,256,1792]{2,1,0:T(8,128)} %fusion.15, bf16[256,2,4096]{2,0,1:T(8,128)(2,1)} %all-gather.2.cloned.1.call-done, bf16[2,4096,1792]{2,1,0:T(8,128)(2,1)} %param.12), kind=kOutput, calls=%fused_computation.2 | convolution fusion | flops 15039987712 | bytes 70778880 | tf_op jit(solution)/shard_map/ref,efd->red/dot_general | solution.py:18
  121.9 0.0 reduce-scatter.2.cloned.1.call-update
  121.9 48.9 %reduce-scatter.2.cloned.1.call-done = bf16[32,2,4096]{2,0,1:T(8,128)(2,1)} async-done(((bf16[256,2,4096]{2,0,1:T(8,128)(2,1)}), bf16[32,2,4096]{2,0,1:T(8,128)(2,1)}) %reduce-scatter.2.cloned.1.call-update) | async-done | bytes 524304 | tf_op jit(solution)/shard_map/reduce_scatter | solution.py:48
  170.8 2.4 %copy.10 = bf16[4,8,2,4096]{3,2,1,0:T(2,128)(2,1)} copy(bf16[4,8,2,4096]{3,1,0,2:T(8,128)(2,1)} %bitcast.47) | data formatting | bytes 1048576 | tf_op jit(solution)/shard_map/reshape | solution.py:51
  173.2 3.6 %all-to-all-start.1 = ((bf16[4,8,2,4096]{3,2,1,0:T(2,128)(2,1)}), bf16[4,8,2,4096]{3,2,1,0:T(2,128)(2,1)S(1)}, u32[]{:S(2)}, u32[]{:S(2)}) async-start(bf16[4,8,2,4096]{3,2,1,0:T(2,128)(2,1)} %copy.10), calls=%async_computation.2 | async-start | bytes 1048576 | tf_op jit(solution)/shard_map/all_to_all | solution.py:52
  176.9 0.0 copy-done
  176.9 0.7 gather_fusion
  177.6 5.9 %all-to-all-done.1 = bf16[4,8,2,4096]{3,2,1,0:T(2,128)(2,1)S(1)} async-done(((bf16[4,8,2,4096]{3,2,1,0:T(2,128)(2,1)}), bf16[4,8,2,4096]{3,2,1,0:T(2,128)(2,1)S(1)}, u32[]{:S(2)}, u32[]{:S(2)}) %all-to-all-start.1) | async-done | bytes 524320 | tf_op jit(solution)/shard_map/all_to_all | solution.py:52
  183.5 0.2 reshape.33
  183.7 1.0 convolution_convert_fusion.2
  (5 shorter events, 0.0 us)
Async XLA Ops:
  6.5 66.8 %all-gather.2.cloned.1.call-start = ((), (), s32[]{:S(2)}) async-start(), calls=%async_computation.3 | async-start | bytes 4718592 | tf_op jit(solution)/shard_map/all_gather | solution.py:46
  26.3 144.6 %reduce-scatter.2.cloned.1.call-start = ((), (), s32[]{:S(2)}) async-start(), calls=%async_computation.4 | async-start | bytes 4718592 | tf_op jit(solution)/shard_map/reduce_scatter | solution.py:48
  121.9 55.0 %copy-start = (s32[32]{0:T(128)S(1)}, s32[32]{0:T(128)}, u32[]{:S(2)}) copy-start(s32[32]{0:T(128)} %param.10) | copy-start | bytes 388
  173.2 10.2 %all-to-all-start.1 = ((bf16[4,8,2,4096]{3,2,1,0:T(2,128)(2,1)}), bf16[4,8,2,4096]{3,2,1,0:T(2,128)(2,1)S(1)}, u32[]{:S(2)}, u32[]{:S(2)}) async-start(bf16[4,8,2,4096]{3,2,1,0:T(2,128)(2,1)} %copy.10), calls=%async_computation.2 | async-start | bytes 1048576 | tf_op jit(solution)/shard_map/all_to_all | solution.py:52
Sparse Core Ops, SparseCore 0:
  26.4 46.8 all-gather.1
  122.1 48.7 reduce-scatter.1
where the time goes:
time: 192 us; the launch traced here: 191 us
  waiting for transfers between devices  102 us (53%)
  matrix products  51 us (27%)
  blocking collectives  13.5 us (7%)
  between operations  13.4 us (7%)
  local copies, waits for them, and re-layouts  4.72 us (2%)
  starting transfers between devices  3.69 us (2%)
  other arithmetic  3.43 us (2%)
    reduce_scatter x1, waiting for transfers between devices, shards(): lax.psum_scatter(partial_terms.astype(jnp.bfloat16), 'shard', scatter_dim...  48.9 us
    all_gather x1, waiting for transfers between devices, shards(): lax.all_gather(local_rows, 'shard', axis=0, tiled=True)  47 us
    dot_general x1, matrix products, expert_block(): jnp.einsum('ref,efd->red', hidden, w_down, preferred_element_type=jnp.flo...  31.8 us
    dot_general x1, matrix products, expert_block(): jnp.einsum('red,edf->ref', gathered_rows, w_gate, preferred_element_type=...  16.8 us
    all_to_all x1, blocking collectives, shards(): lax.all_to_all(outgoing, 'task', split_axis=0, concat_axis=0, tiled=True)  13.5 us
    all_to_all x1, waiting for transfers between devices, shards(): lax.all_to_all(results, 'task', split_axis=0, concat_axis=0, tiled=True)  5.85 us
  transfers between devices with their start and end apart: 3, of which 3 were waited for; matrix products, arithmetic and copies ran while one was open for 0% of the time, Pallas kernels for 0%

commit v1 on v0

--- a/solution.py
+++ b/solution.py
@@ -1,12 +1,345 @@
+import functools
+
 import jax
 import jax.numpy as jnp
 from jax import lax
+from jax.experimental import pallas as pl
+from jax.experimental.pallas import tpu as pltpu
 from jax.sharding import PartitionSpec as P
 
+MESH = pl.DeviceIdType.MESH
 CAP = 8
-
-
+CORES = 2
+CHUNK = 1024
+UP_SLOTS = 6
+DOWN_SLOTS = 3
+VMEM_BYTES = 63 * 2**20
 epsilon = 1e-06
+
+
+def tile_of(size):
+    return 256 if size % 256 == 0 else size
+
+
+def layer_kernel(
+    tasks, chips, chunk,
+    tokens, gain, task_col, task_row, order_col, w_gate, w_up, w_down, out,
+    ids, rows, placed, x, gate_acc, up_acc, hidden, part, sib, pair, back, picked, terms, wbuf, dbuf,
+    w_sem, d_sem, i_send, i_recv, z_send, z_recv, x_send, x_recv, x_local, b_send, b_recv,
+    c_send, c_recv, y_send, y_recv, y_local, t_send, t_recv,
+):
+    experts, width, ff = w_gate.shape
+    count = tokens.shape[0]
+    chunks = width // chunk
+    per = chips * CAP
+    slots = tasks * experts * per
+    tile = tile_of(ff)
+    me_t = lax.axis_index("task")
+    me_s = lax.axis_index("shard")
+    me_q = me_s // CORES
+    me_c = me_s % CORES
+    other_c = 1 - me_c
+    sibling = (me_t, me_q * CORES + other_c)
+
+    def chip_at(k):
+        return lax.rem(me_q + k, chips)
+
+    def task_at(k):
+        return lax.rem(me_t + k, tasks)
+
+    up_pieces = [(j, e, w) for j in range(chunks) for e in range(experts) for w in (w_gate, w_up)]
+    down_pieces = [(j, e) for j in range(chunks) for e in range(experts)]
+
+    def up_copy(i):
+        j, e, w = up_pieces[i]
+        slot = i % UP_SLOTS
+        return pltpu.make_async_copy(
+            w.at[e, pl.ds(j * chunk, chunk), :], wbuf.at[slot], w_sem.at[slot]
+        )
+
+    def down_copy(i):
+        j, e = down_pieces[i]
+        slot = i % DOWN_SLOTS
+        return pltpu.make_async_copy(
+            w_down.at[e, :, pl.ds(j * chunk, chunk)], dbuf.at[slot], d_sem.at[slot]
+        )
+
+    barrier = pltpu.get_barrier_semaphore()
+    chip_peers = [(me_t, chip_at(k) * CORES + me_c) for k in range(1, chips)]
+    task_peers = [(task_at(k), me_s) for k in range(1, tasks)]
+    for peer in chip_peers + task_peers + [sibling]:
+        pl.semaphore_signal(barrier, inc=1, device_id=peer, device_id_type=MESH)
+
+    for i in range(min(UP_SLOTS, len(up_pieces))):
+        up_copy(i).start()
+    for i in range(min(DOWN_SLOTS, len(down_pieces))):
+        down_copy(i).start()
+
+    col = jnp.broadcast_to(task_col[...], (count, count))
+    row = jnp.broadcast_to(task_row[...], (count, count))
+    first = lax.broadcasted_iota(jnp.int32, (count, count), 0)
+    second = lax.broadcasted_iota(jnp.int32, (count, count), 1)
+    same = col == row
+    col_pos = jnp.sum(jnp.where(same & (second < first), 1.0, 0.0), axis=1, keepdims=True)
+    row_pos = jnp.sum(jnp.where(same & (first < second), 1.0, 0.0), axis=0, keepdims=True)
+    col_id = task_col[...].astype(jnp.float32) * CAP + col_pos
+    row_id = task_row[...].astype(jnp.float32) * CAP + row_pos
+    taken = jnp.broadcast_to(order_col[...], (count, count)) == second
+    want_id = jnp.sum(
+        jnp.where(taken, jnp.broadcast_to(row_id, (count, count)), 0.0), axis=1, keepdims=True
+    )
+    ids[me_q, 0] = jnp.broadcast_to(col_id, (count, 128))
+    ids[me_q, 1] = jnp.broadcast_to(want_id, (count, 128))
+
+    values = tokens[...].astype(jnp.float32)
+    mean_square = jnp.mean(values * values, axis=-1, keepdims=True)
+    scale = lax.rsqrt(mean_square + epsilon)
+    for j in range(chunks):
+        part_cols = pl.ds(j * chunk, chunk)
+        rows[j, me_q] = (
+            tokens[:, part_cols].astype(jnp.float32) * scale * gain[:, part_cols]
+        ).astype(jnp.bfloat16)
+
+    pl.semaphore_wait(barrier, len(chip_peers) + len(task_peers) + 1)
+
+    sends = []
+
+    def remote(src, dst, send, recv, peer):
+        copy = pltpu.make_async_remote_copy(
+            src_ref=src, dst_ref=dst, send_sem=send, recv_sem=recv,
+            device_id=peer, device_id_type=MESH,
+        )
+        copy.start()
+        sends.append(copy)
+        return copy
+
+    id_copies = [
+        remote(ids.at[me_q], ids.at[me_q], i_send.at[k], i_recv.at[k], peer)
+        for k, peer in enumerate(chip_peers)
+    ]
+    row_copies = [
+        [
+            remote(rows.at[j, me_q], rows.at[j, me_q], z_send.at[j, k], z_recv.at[j, k], peer)
+            for k, peer in enumerate(chip_peers)
+        ]
+        for j in range(chunks)
+    ]
+
+    for copy in id_copies:
+        copy.wait_recv()
+    shape = (chips * count, slots)
+    lane = lax.broadcasted_iota(jnp.int32, shape, 1)
+    line = lax.broadcasted_iota(jnp.int32, shape, 0)
+    lane_id = ((lane // per) * CAP + lane % CAP).astype(jnp.float32)
+    mine = (lane // CAP) % chips == line // count
+
+    def one_hot(which):
+        held = ids[:, which].reshape(chips * count, 128)[:, :1]
+        hit = (jnp.broadcast_to(held, shape) == lane_id) & mine
+        return jnp.where(hit, 1.0, 0.0)
+
+    placing = one_hot(0).T.astype(jnp.bfloat16)
+    picking = one_hot(1).astype(jnp.bfloat16)
+
+    cross, swaps, pair_swaps, returns, finals = {}, {}, {}, {}, {}
+
+    def place(j):
+        for copy in row_copies[j]:
+            copy.wait_recv()
+        for n in range(0, chunk, 256):
+            got = jnp.dot(
+                placing,
+                rows[j, :, :, n : n + 256].reshape(chips * count, 256),
+                preferred_element_type=jnp.float32,
+            ).astype(jnp.bfloat16)
+            placed[j, :, :, :, n : n + 256] = got.reshape(tasks, experts, per, 256)
+        cross[j] = [
+            remote(
+                placed.at[j, peer[0]], x.at[j, :, me_c, me_t],
+                x_send.at[j, k], x_recv.at[j, k], peer,
+            )
+            for k, peer in enumerate(task_peers)
+        ]
+        local = pltpu.make_async_copy(
+            placed.at[j, me_t], x.at[j, :, me_c, me_t], x_local.at[j]
+        )
+        local.start()
+        cross[j].append(local)
+
+    def swap(j):
+        for copy in cross[j][:-1]:
+            copy.wait_recv()
+        cross[j][-1].wait()
+        swaps[j] = remote(
+            x.at[j, :, me_c], x.at[j, :, me_c], b_send.at[j], b_recv.at[j], sibling
+        )
+
+    def enter(j):
+        swaps[j].wait_recv()
+        for e in range(experts):
+            i = (j * experts + e) * 2
+            up_copy(i).wait()
+            up_copy(i + 1).wait()
+
+            def step(n, carry):
+                columns = pl.ds(pl.multiple_of(n * tile, tile), tile)
+                block = x[j, e].reshape(CORES * tasks * per, chunk)
+                g = jnp.dot(
+                    block, wbuf[i % UP_SLOTS, :, columns], preferred_element_type=jnp.float32
+                )
+                u = jnp.dot(
+                    block, wbuf[(i + 1) % UP_SLOTS, :, columns], preferred_element_type=jnp.float32
+                )
+                if j > 0:
+                    g += gate_acc[e, :, columns]
+                    u += up_acc[e, :, columns]
+                if j < chunks - 1:
+                    gate_acc[e, :, columns] = g
+                    up_acc[e, :, columns] = u
+                else:
+                    hidden[e, :, columns] = (g / (1.0 + jnp.exp(-g)) * u).astype(jnp.bfloat16)
+                return carry
+
+            lax.fori_loop(0, ff // tile, step, 0)
+            for later in (i + UP_SLOTS, i + 1 + UP_SLOTS):
+                if later < len(up_pieces):
+                    up_copy(later).start()
+
+    def leave(j):
+        for e in range(experts):
+            i = j * experts + e
+            down_copy(i).wait()
+
+            def step(n, carry):
+                columns = pl.ds(pl.multiple_of(n * 256, 256), 256)
+                got = jnp.dot(
+                    hidden[e], dbuf[i % DOWN_SLOTS, :, columns], preferred_element_type=jnp.float32
+                ).astype(jnp.bfloat16)
+                part[j, e, :, :, :, columns] = got.reshape(CORES, tasks, per, 256)
+                return carry
+
+            lax.fori_loop(0, chunk // 256, step, 0)
+            if i + DOWN_SLOTS < len(down_pieces):
+                down_copy(i + DOWN_SLOTS).start()
+        pair_swaps[j] = remote(
+            part.at[j, :, other_c], sib.at[j], c_send.at[j], c_recv.at[j], sibling
+        )
+
+    def add_pair(j):
+        pair_swaps[j].wait_recv()
+        for e in range(experts):
+            for t in range(tasks):
+                pair[j, e, t] = (
+                    part[j, e, me_c, t].astype(jnp.float32) + sib[j, e, t].astype(jnp.float32)
+                ).astype(jnp.bfloat16)
+        returns[j] = [
+            remote(
+                pair.at[j, :, peer[0]], back.at[j, me_t], y_send.at[j, k], y_recv.at[j, k], peer
+            )
+            for k, peer in enumerate(task_peers)
+        ]
+        local = pltpu.make_async_copy(pair.at[j, :, me_t], back.at[j, me_t], y_local.at[j])
+        local.start()
+        returns[j].append(local)
+
+    def pick(j):
+        for copy in returns[j][:-1]:
+            copy.wait_recv()
+        returns[j][-1].wait()
+        for n in range(0, chunk, 256):
+            got = jnp.dot(
+                picking,
+                back[j, :, :, :, n : n + 256].reshape(slots, 256),
+                preferred_element_type=jnp.float32,
+            ).astype(jnp.bfloat16)
+            picked[j, :, :, n : n + 256] = got.reshape(chips, count, 256)
+        finals[j] = [
+            remote(
+                picked.at[j, chip_at(k + 1)], terms.at[j, me_q],
+                t_send.at[j, k], t_recv.at[j, k], peer,
+            )
+            for k, peer in enumerate(chip_peers)
+        ]
+        terms[j, me_q] = picked[j, me_q]
+
+    def finish(j):
+        for copy in finals[j]:
+            copy.wait_recv()
+        total = terms[j, 0].astype(jnp.float32)
+        for k in range(1, chips):
+            total += terms[j, k].astype(jnp.float32)
+        out[:, pl.ds(j * chunk, chunk)] = total.astype(jnp.bfloat16)
+
+    for step in range(chunks + 2):
+        if step < chunks:
+            place(step)
+        if 0 <= step - 1 < chunks:
+            swap(step - 1)
+        if 0 <= step - 2 < chunks:
+            enter(step - 2)
+    for step in range(chunks + 3):
+        if step < chunks:
+            leave(step)
+        if 0 <= step - 1 < chunks:
+            add_pair(step - 1)
+        if 0 <= step - 2 < chunks:
+            pick(step - 2)
+        if 0 <= step - 3 < chunks:
+            finish(step - 3)
+    for copy in sends:
+        copy.wait_send()
+
+
+def scratch_of(tasks, chips, chunk, tokens, w_gate):
+    experts, width, ff = w_gate.shape
+    count = tokens.shape[0]
+    chunks, per = width // chunk, chips * CAP
+    bf16, f32 = jnp.bfloat16, jnp.float32
+    group = CORES * tasks * per
+    buffers = [
+        ((chips, 2, count, 128), f32),
+        ((chunks, chips, count, chunk), bf16),
+        ((chunks, tasks, experts, per, chunk), bf16),
+        ((chunks, experts, CORES, tasks, per, chunk), bf16),
+        ((experts, group, ff), f32),
+        ((experts, group, ff), f32),
+        ((experts, group, ff), bf16),
+        ((chunks, experts, CORES, tasks, per, chunk), bf16),
+        ((chunks, experts, tasks, per, chunk), bf16),
+        ((chunks, experts, tasks, per, chunk), bf16),
+        ((chunks, tasks, experts, per, chunk), bf16),
+        ((chunks, chips, count, chunk), bf16),
+        ((chunks, chips, count, chunk), bf16),
+        ((UP_SLOTS, chunk, ff), bf16),
+        ((DOWN_SLOTS, ff, chunk), bf16),
+    ]
+    size = sum(functools.reduce(lambda a, b: a * b, s) * jnp.dtype(d).itemsize for s, d in buffers)
+    dma = pltpu.SemaphoreType.DMA
+    sems = [dma((UP_SLOTS,)), dma((DOWN_SLOTS,)), dma((chips,)), dma((chips,))]
+    sems += [dma((chunks, chips))] * 2 + [dma((chunks, tasks))] * 2 + [dma((chunks,))] * 5
+    sems += [dma((chunks, tasks))] * 2 + [dma((chunks,))] + [dma((chunks, chips))] * 2
+    return [pltpu.VMEM(s, d) for s, d in buffers] + sems, size
+
+
+def fused(tokens, gain, task_ids, order, w_gate, w_up, w_down, scratch, chunk):
+    tasks, chips = lax.axis_size("task"), lax.axis_size("shard") // CORES
+    count, width = tokens.shape
+    vmem = pl.BlockSpec(memory_space=pltpu.VMEM)
+    hbm = pl.BlockSpec(memory_space=pl.ANY)
+    return pl.pallas_call(
+        functools.partial(layer_kernel, tasks, chips, chunk),
+        out_shape=jax.ShapeDtypeStruct((count, width), jnp.bfloat16),
+        in_specs=[vmem] * 5 + [hbm] * 3,
+        out_specs=vmem,
+        scratch_shapes=scratch,
+        compiler_params=pltpu.CompilerParams(
+            collective_id=0, has_side_effects=True, vmem_limit_bytes=VMEM_BYTES
+        ),
+        name="expert_layer",
+    )(
+        tokens, gain.reshape(1, width), task_ids.reshape(count, 1), task_ids.reshape(1, count),
+        order.reshape(count, 1), w_gate, w_up, w_down,
+    )
 
 
 def expert_block(gathered_rows, w_gate, w_up, w_down):
@@ -18,7 +351,7 @@
     return jnp.einsum("ref,efd->red", hidden, w_down, preferred_element_type=jnp.float32)
 
 
-def shards(tokens, gain, task_ids, order, w_gate, w_up, w_down):
+def collective(tokens, gain, task_ids, order, w_gate, w_up, w_down):
     task_count = lax.axis_size("task")
     local_experts = w_gate.shape[0]
     expert_count = task_count * local_experts
@@ -56,6 +389,18 @@
     return jnp.dot(selecting, returned, preferred_element_type=jnp.float32).astype(jnp.bfloat16)
 
 
+def shards(tokens, gain, task_ids, order, w_gate, w_up, w_down):
+    tasks, shard_count = lax.axis_size("task"), lax.axis_size("shard")
+    width = tokens.shape[1]
+    chunk = CHUNK if width % CHUNK == 0 else width
+    chips = shard_count // CORES
+    scratch, size = scratch_of(tasks, chips, chunk, tokens, w_gate)
+    arrays = (tokens, gain, task_ids, order, w_gate, w_up, w_down)
+    if shard_count % CORES or chunk % 256 or size + 2 * 2**20 > VMEM_BYTES:
+        return collective(*arrays)
+    return fused(*arrays, scratch, chunk)
+
+
 def solution(mesh):
     placed = (
         P(("task", "shard"), None),

time: 192 us -> 106 us (0.55)
  Pallas kernels: 0 us -> 102 us
  waiting for transfers between devices: 102 us -> 0 us
  matrix products: 51 us -> 0 us
  blocking collectives: 13.5 us -> 0 us
  between operations: 13.4 us -> 0.01 us
  starting transfers between devices: 3.69 us -> 0 us
  other arithmetic: 3.43 us -> 0 us
    pallas_call x0 -> x1, Pallas kernels: none -> 102 us  [fused(): pl.pallas_call(functools.partial(layer_kernel, tasks, chips, chunk), out_...]
    dot_general x4 -> x0, matrix products: 51 us -> none  [the longest x1 31.8 us: expert_block(): jnp.einsum('ref,efd->red', hidden, w_down, preferred_element_type=jnp.flo...]
    reduce_scatter x1 -> x0, waiting for transfers between devices: 48.9 us -> none  [shards(): lax.psum_scatter(partial_terms.astype(jnp.bfloat16), 'shard', scatter_dim...]
    all_gather x1 -> x0, waiting for transfers between devices: 47 us -> none  [shards(): lax.all_gather(local_rows, 'shard', axis=0, tiled=True)]
    all_to_all x1 -> x0, blocking collectives: 13.5 us -> none  [shards(): lax.all_to_all(outgoing, 'task', split_axis=0, concat_axis=0, tiled=True)]
    all_to_all x1 -> x0, waiting for transfers between devices: 5.85 us -> none  [shards(): lax.all_to_all(results, 'task', split_axis=0, concat_axis=0, tiled=True)]
    all_to_all x1 -> x0, starting transfers between devices: 3.65 us -> none  [shards(): lax.all_to_all(results, 'task', split_axis=0, concat_axis=0, tiled=True)]
    reduce_sum x2 -> x0, other arithmetic: 1.94 us -> none  [the longest x1 1.11 us: shards(): mean_square = jnp.mean(values * values, axis=-1, keepdims=True)]
  transfers between devices with their start and end apart: 3 -> 0, of which waited for: 3 -> 0; matrix products, arithmetic and copies ran while one was open for 0% -> 0% of each run, Pallas kernels for 0% -> 0%
where the time goes in v1:
time: 106 us
  Pallas kernels  102 us (96%)
  local copies, waits for them, and re-layouts  4.34 us (4%)
    pallas_call x1, Pallas kernels, fused(): pl.pallas_call(functools.partial(layer_kernel, tasks, chips, chunk), out_...  102 us

profile of v1, /device:TPU:0, one launch (start us, length us, event | category | flops | bytes accessed | tf_op | source)
XLA Modules:
  0.0 106.2 jit_solution(14328534851649645491)
XLA Ops:
  0.0 1.3 %copy.9.order_col = s32[32,1]{1,0:T(8,128)} copy(s32[32,1]{0,1:T(1,128)} %bitcast.7) | data formatting | bytes 256 | tf_op jit(solution)/shard_map/reshape | solution.py:341
  1.3 1.3 %copy.8.task_col = s32[32,1]{1,0:T(8,128)} copy(s32[32,1]{0,1:T(1,128)} %bitcast.5) | data formatting | bytes 256 | tf_op jit(solution)/shard_map/reshape | solution.py:340
  2.7 101.9 %expert_layer.1 = bf16[32,4096]{1,0:T(8,128)(2,1)} custom-call(bf16[32,4096]{1,0:T(8,128)(2,1)} %tokens.1, f32[1,4096]{1,0:T(1,128)} %bitcast.4, s32[32,1]{1,0:T(8,128)} %copy.8.task_col, s32[1,32]{1,0:T(1,128)} %bitcast.6, s32[32,1]{1,0:T(8,128)} %copy.9.order_col, bf16[2,4096,1792]{2,1,0:T(8,128)(2,1)} %w_gate.1, bf16[2,4096,1792]{2,1,0:T(8,128)(2,1)} %w_up.1, ...), custom_call_target="tpu_custom_call" | custom-call | tf_op jit(solution)/shard_map/expert_layer/pallas_call | solution.py:329
  104.6 1.7 %copy.11 = bf16[32,4096]{1,0:T(8,128)(2,1)} copy(bf16[32,4096]{1,0:T(8,128)(2,1)} %expert_layer.1) | data formatting | bytes 524288

commit v2 on v1

--- a/solution.py
+++ b/solution.py
@@ -13,6 +13,7 @@
 CHUNK = 1024
 UP_SLOTS = 6
 DOWN_SLOTS = 3
+AHEAD = 2
 VMEM_BYTES = 63 * 2**20
 epsilon = 1e-06
 
@@ -23,7 +24,7 @@
 
 def layer_kernel(
     tasks, chips, chunk,
-    tokens, gain, task_col, task_row, order_col, w_gate, w_up, w_down, out,
+    tokens, gain, task_row, order_row, w_gate, w_up, w_down, out,
     ids, rows, placed, x, gate_acc, up_acc, hidden, part, sib, pair, back, picked, terms, wbuf, dbuf,
     w_sem, d_sem, i_send, i_recv, z_send, z_recv, x_send, x_recv, x_local, b_send, b_recv,
     c_send, c_recv, y_send, y_recv, y_local, t_send, t_recv,
@@ -75,16 +76,25 @@
     for i in range(min(DOWN_SLOTS, len(down_pieces))):
         down_copy(i).start()
 
-    col = jnp.broadcast_to(task_col[...], (count, count))
-    row = jnp.broadcast_to(task_row[...], (count, count))
     first = lax.broadcasted_iota(jnp.int32, (count, count), 0)
     second = lax.broadcasted_iota(jnp.int32, (count, count), 1)
+    task_line = task_row[...].astype(jnp.float32)
+    order_line = order_row[...].astype(jnp.float32)
+
+    def as_column(line):
+        spread = jnp.broadcast_to(line, (count, count))
+        return jnp.sum(jnp.where(first == second, spread, 0.0), axis=1, keepdims=True)
+
+    task_col = as_column(task_line)
+    order_col = as_column(order_line)
+    col = jnp.broadcast_to(task_col, (count, count))
+    row = jnp.broadcast_to(task_line, (count, count))
     same = col == row
     col_pos = jnp.sum(jnp.where(same & (second < first), 1.0, 0.0), axis=1, keepdims=True)
     row_pos = jnp.sum(jnp.where(same & (first < second), 1.0, 0.0), axis=0, keepdims=True)
-    col_id = task_col[...].astype(jnp.float32) * CAP + col_pos
-    row_id = task_row[...].astype(jnp.float32) * CAP + row_pos
-    taken = jnp.broadcast_to(order_col[...], (count, count)) == second
+    col_id = task_col * CAP + col_pos
+    row_id = task_line * CAP + row_pos
+    taken = jnp.broadcast_to(order_col, (count, count)) == second.astype(jnp.float32)
     want_id = jnp.sum(
         jnp.where(taken, jnp.broadcast_to(row_id, (count, count)), 0.0), axis=1, keepdims=True
     )
@@ -117,13 +127,16 @@
         remote(ids.at[me_q], ids.at[me_q], i_send.at[k], i_recv.at[k], peer)
         for k, peer in enumerate(chip_peers)
     ]
-    row_copies = [
-        [
+    row_copies = {}
+
+    def send_rows(j):
+        row_copies[j] = [
             remote(rows.at[j, me_q], rows.at[j, me_q], z_send.at[j, k], z_recv.at[j, k], peer)
             for k, peer in enumerate(chip_peers)
         ]
-        for j in range(chunks)
-    ]
+
+    for j in range(min(AHEAD, chunks)):
+        send_rows(j)
 
     for copy in id_copies:
         copy.wait_recv()
@@ -146,6 +159,8 @@
     def place(j):
         for copy in row_copies[j]:
             copy.wait_recv()
+        if j + AHEAD < chunks:
+            send_rows(j + AHEAD)
         for n in range(0, chunk, 256):
             got = jnp.dot(
                 placing,
@@ -329,7 +344,7 @@
     return pl.pallas_call(
         functools.partial(layer_kernel, tasks, chips, chunk),
         out_shape=jax.ShapeDtypeStruct((count, width), jnp.bfloat16),
-        in_specs=[vmem] * 5 + [hbm] * 3,
+        in_specs=[vmem] * 4 + [hbm] * 3,
         out_specs=vmem,
         scratch_shapes=scratch,
         compiler_params=pltpu.CompilerParams(
@@ -337,8 +352,8 @@
         ),
         name="expert_layer",
     )(
-        tokens, gain.reshape(1, width), task_ids.reshape(count, 1), task_ids.reshape(1, count),
-        order.reshape(count, 1), w_gate, w_up, w_down,
+        tokens, gain.reshape(1, width), task_ids.reshape(1, count), order.reshape(1, count),
+        w_gate, w_up, w_down,
     )
 
 

time: 106 us -> 103 us (0.972)
  local copies, waits for them, and re-layouts: 4.34 us -> 1.67 us
    reshape x2 -> x0, local copies, waits for them, and re-layouts: 2.67 us -> none  [the longest x1 1.34 us: fused(): task_ids.reshape(count, 1)]
where the time goes in v2:
time: 103 us
  Pallas kernels  102 us (99%)
  local copies, waits for them, and re-layouts  1.67 us (2%)
    pallas_call x1, Pallas kernels, fused(): pl.pallas_call(functools.partial(layer_kernel, tasks, chips, chunk), out_...  102 us

profile of v2, /device:TPU:0, one launch (start us, length us, event | category | flops | bytes accessed | tf_op | source)
XLA Modules:
  0.0 103.2 jit_solution(14992722682996755421)
XLA Ops:
  0.0 101.5 %expert_layer.1 = bf16[32,4096]{1,0:T(8,128)(2,1)} custom-call(bf16[32,4096]{1,0:T(8,128)(2,1)} %tokens.1, f32[1,4096]{1,0:T(1,128)} %bitcast.3, s32[1,32]{1,0:T(1,128)} %bitcast.4, s32[1,32]{1,0:T(1,128)} %bitcast.5, bf16[2,4096,1792]{2,1,0:T(8,128)(2,1)} %w_gate.1, bf16[2,4096,1792]{2,1,0:T(8,128)(2,1)} %w_up.1, bf16[2,1792,4096]{2,1,0:T(8,128)(2,1)} %w_down.1), custom_call_target="tpu_custom_call" | custom-call | tf_op jit(solution)/shard_map/expert_layer/pallas_call | solution.py:344
  101.5 1.7 %copy.9 = bf16[32,4096]{1,0:T(8,128)(2,1)} copy(bf16[32,4096]{1,0:T(8,128)(2,1)} %expert_layer.1) | data formatting | bytes 524288

commit v3 on v2

--- a/solution.py
+++ b/solution.py
@@ -11,9 +11,11 @@
 CAP = 8
 CORES = 2
 CHUNK = 1024
+OUT_CHUNK = 512
 UP_SLOTS = 6
-DOWN_SLOTS = 3
+DOWN_SLOTS = 6
 AHEAD = 2
+EARLY = 4
 VMEM_BYTES = 63 * 2**20
 epsilon = 1e-06
 
@@ -23,7 +25,7 @@
 
 
 def layer_kernel(
-    tasks, chips, chunk,
+    tasks, chips, chunk, out_chunk,
     tokens, gain, task_row, order_row, w_gate, w_up, w_down, out,
     ids, rows, placed, x, gate_acc, up_acc, hidden, part, sib, pair, back, picked, terms, wbuf, dbuf,
     w_sem, d_sem, i_send, i_recv, z_send, z_recv, x_send, x_recv, x_local, b_send, b_recv,
@@ -32,6 +34,7 @@
     experts, width, ff = w_gate.shape
     count = tokens.shape[0]
     chunks = width // chunk
+    out_chunks = width // out_chunk
     per = chips * CAP
     slots = tasks * experts * per
     tile = tile_of(ff)
@@ -49,7 +52,7 @@
         return lax.rem(me_t + k, tasks)
 
     up_pieces = [(j, e, w) for j in range(chunks) for e in range(experts) for w in (w_gate, w_up)]
-    down_pieces = [(j, e) for j in range(chunks) for e in range(experts)]
+    down_pieces = [(j, e) for j in range(out_chunks) for e in range(experts)]
 
     def up_copy(i):
         j, e, w = up_pieces[i]
@@ -62,7 +65,7 @@
         j, e = down_pieces[i]
         slot = i % DOWN_SLOTS
         return pltpu.make_async_copy(
-            w_down.at[e, :, pl.ds(j * chunk, chunk)], dbuf.at[slot], d_sem.at[slot]
+            w_down.at[e, :, pl.ds(j * out_chunk, out_chunk)], dbuf.at[slot], d_sem.at[slot]
         )
 
     barrier = pltpu.get_barrier_semaphore()
@@ -71,10 +74,8 @@
     for peer in chip_peers + task_peers + [sibling]:
         pl.semaphore_signal(barrier, inc=1, device_id=peer, device_id_type=MESH)
 
-    for i in range(min(UP_SLOTS, len(up_pieces))):
+    for i in range(min(EARLY, UP_SLOTS, len(up_pieces))):
         up_copy(i).start()
-    for i in range(min(DOWN_SLOTS, len(down_pieces))):
-        down_copy(i).start()
 
     first = lax.broadcasted_iota(jnp.int32, (count, count), 0)
     second = lax.broadcasted_iota(jnp.int32, (count, count), 1)
@@ -137,6 +138,11 @@
 
     for j in range(min(AHEAD, chunks)):
         send_rows(j)
+
+    for i in range(EARLY, min(UP_SLOTS, len(up_pieces))):
+        up_copy(i).start()
+    for i in range(min(DOWN_SLOTS, len(down_pieces))):
+        down_copy(i).start()
 
     for copy in id_copies:
         copy.wait_recv()
@@ -225,15 +231,10 @@
             i = j * experts + e
             down_copy(i).wait()
 
-            def step(n, carry):
-                columns = pl.ds(pl.multiple_of(n * 256, 256), 256)
-                got = jnp.dot(
-                    hidden[e], dbuf[i % DOWN_SLOTS, :, columns], preferred_element_type=jnp.float32
-                ).astype(jnp.bfloat16)
-                part[j, e, :, :, :, columns] = got.reshape(CORES, tasks, per, 256)
-                return carry
-
-            lax.fori_loop(0, chunk // 256, step, 0)
+            got = jnp.dot(
+                hidden[e], dbuf[i % DOWN_SLOTS], preferred_element_type=jnp.float32
+            ).astype(jnp.bfloat16)
+            part[j, e] = got.reshape(CORES, tasks, per, out_chunk)
             if i + DOWN_SLOTS < len(down_pieces):
                 down_copy(i + DOWN_SLOTS).start()
         pair_swaps[j] = remote(
@@ -261,7 +262,7 @@
         for copy in returns[j][:-1]:
             copy.wait_recv()
         returns[j][-1].wait()
-        for n in range(0, chunk, 256):
+        for n in range(0, out_chunk, 256):
             got = jnp.dot(
                 picking,
                 back[j, :, :, :, n : n + 256].reshape(slots, 256),
@@ -283,7 +284,7 @@
         total = terms[j, 0].astype(jnp.float32)
         for k in range(1, chips):
             total += terms[j, k].astype(jnp.float32)
-        out[:, pl.ds(j * chunk, chunk)] = total.astype(jnp.bfloat16)
+        out[:, pl.ds(j * out_chunk, out_chunk)] = total.astype(jnp.bfloat16)
 
     for step in range(chunks + 2):
         if step < chunks:
@@ -292,23 +293,23 @@
             swap(step - 1)
         if 0 <= step - 2 < chunks:
             enter(step - 2)
-    for step in range(chunks + 3):
-        if step < chunks:
+    for step in range(out_chunks + 3):
+        if step < out_chunks:
             leave(step)
-        if 0 <= step - 1 < chunks:
+        if 0 <= step - 1 < out_chunks:
             add_pair(step - 1)
-        if 0 <= step - 2 < chunks:
+        if 0 <= step - 2 < out_chunks:
             pick(step - 2)
-        if 0 <= step - 3 < chunks:
+        if 0 <= step - 3 < out_chunks:
             finish(step - 3)
     for copy in sends:
         copy.wait_send()
 
 
-def scratch_of(tasks, chips, chunk, tokens, w_gate):
+def scratch_of(tasks, chips, chunk, out_chunk, tokens, w_gate):
     experts, width, ff = w_gate.shape
     count = tokens.shape[0]
-    chunks, per = width // chunk, chips * CAP
+    chunks, out_chunks, per = width // chunk, width // out_chunk, chips * CAP
     bf16, f32 = jnp.bfloat16, jnp.float32
     group = CORES * tasks * per
     buffers = [
@@ -319,30 +320,31 @@
         ((experts, group, ff), f32),
         ((experts, group, ff), f32),
         ((experts, group, ff), bf16),
-        ((chunks, experts, CORES, tasks, per, chunk), bf16),
-        ((chunks, experts, tasks, per, chunk), bf16),
-        ((chunks, experts, tasks, per, chunk), bf16),
-        ((chunks, tasks, experts, per, chunk), bf16),
-        ((chunks, chips, count, chunk), bf16),
-        ((chunks, chips, count, chunk), bf16),
+        ((out_chunks, experts, CORES, tasks, per, out_chunk), bf16),
+        ((out_chunks, experts, tasks, per, out_chunk), bf16),
+        ((out_chunks, experts, tasks, per, out_chunk), bf16),
+        ((out_chunks, tasks, experts, per, out_chunk), bf16),
+        ((out_chunks, chips, count, out_chunk), bf16),
+        ((out_chunks, chips, count, out_chunk), bf16),
         ((UP_SLOTS, chunk, ff), bf16),
-        ((DOWN_SLOTS, ff, chunk), bf16),
+        ((DOWN_SLOTS, ff, out_chunk), bf16),
     ]
     size = sum(functools.reduce(lambda a, b: a * b, s) * jnp.dtype(d).itemsize for s, d in buffers)
     dma = pltpu.SemaphoreType.DMA
     sems = [dma((UP_SLOTS,)), dma((DOWN_SLOTS,)), dma((chips,)), dma((chips,))]
-    sems += [dma((chunks, chips))] * 2 + [dma((chunks, tasks))] * 2 + [dma((chunks,))] * 5
-    sems += [dma((chunks, tasks))] * 2 + [dma((chunks,))] + [dma((chunks, chips))] * 2
+    sems += [dma((chunks, chips))] * 2 + [dma((chunks, tasks))] * 2 + [dma((chunks,))] * 3
+    sems += [dma((out_chunks,))] * 2 + [dma((out_chunks, tasks))] * 2
+    sems += [dma((out_chunks,))] + [dma((out_chunks, chips))] * 2
     return [pltpu.VMEM(s, d) for s, d in buffers] + sems, size
 
 
-def fused(tokens, gain, task_ids, order, w_gate, w_up, w_down, scratch, chunk):
+def fused(tokens, gain, task_ids, order, w_gate, w_up, w_down, scratch, chunk, out_chunk):
     tasks, chips = lax.axis_size("task"), lax.axis_size("shard") // CORES
     count, width = tokens.shape
     vmem = pl.BlockSpec(memory_space=pltpu.VMEM)
     hbm = pl.BlockSpec(memory_space=pl.ANY)
     return pl.pallas_call(
-        functools.partial(layer_kernel, tasks, chips, chunk),
+        functools.partial(layer_kernel, tasks, chips, chunk, out_chunk),
         out_shape=jax.ShapeDtypeStruct((count, width), jnp.bfloat16),
         in_specs=[vmem] * 4 + [hbm] * 3,
         out_specs=vmem,
@@ -408,12 +410,13 @@
     tasks, shard_count = lax.axis_size("task"), lax.axis_size("shard")
     width = tokens.shape[1]
     chunk = CHUNK if width % CHUNK == 0 else width
+    out_chunk = OUT_CHUNK if width % OUT_CHUNK == 0 else width
     chips = shard_count // CORES
-    scratch, size = scratch_of(tasks, chips, chunk, tokens, w_gate)
+    scratch, size = scratch_of(tasks, chips, chunk, out_chunk, tokens, w_gate)
     arrays = (tokens, gain, task_ids, order, w_gate, w_up, w_down)
-    if shard_count % CORES or chunk % 256 or size + 2 * 2**20 > VMEM_BYTES:
+    if shard_count % CORES or chunk % 256 or out_chunk % 256 or size + 2 * 2**20 > VMEM_BYTES:
         return collective(*arrays)
-    return fused(*arrays, scratch, chunk)
+    return fused(*arrays, scratch, chunk, out_chunk)
 
 
 def solution(mesh):

time: 103 us -> 106 us (1.029)
  Pallas kernels: 102 us -> 104 us
    pallas_call x1, Pallas kernels: 102 us -> 104 us  [fused(): pl.pallas_call(functools.partial(layer_kernel, tasks, chips, chunk, out_c...]
where the time goes in v3:
time: 106 us
  Pallas kernels  104 us (98%)
  local copies, waits for them, and re-layouts  1.67 us (2%)
    pallas_call x1, Pallas kernels, fused(): pl.pallas_call(functools.partial(layer_kernel, tasks, chips, chunk, out_c...  104 us

profile of v3, /device:TPU:0, one launch (start us, length us, event | category | flops | bytes accessed | tf_op | source)
XLA Modules:
  0.0 105.5 jit_solution(3990137341296200161)
XLA Ops:
  0.0 103.8 %expert_layer.1 = bf16[32,4096]{1,0:T(8,128)(2,1)} custom-call(bf16[32,4096]{1,0:T(8,128)(2,1)} %tokens.1, f32[1,4096]{1,0:T(1,128)} %bitcast.3, s32[1,32]{1,0:T(1,128)} %bitcast.4, s32[1,32]{1,0:T(1,128)} %bitcast.5, bf16[2,4096,1792]{2,1,0:T(8,128)(2,1)} %w_gate.1, bf16[2,4096,1792]{2,1,0:T(8,128)(2,1)} %w_up.1, bf16[2,1792,4096]{2,1,0:T(8,128)(2,1)} %w_down.1), custom_call_target="tpu_custom_call" | custom-call | tf_op jit(solution)/shard_map/expert_layer/pallas_call | solution.py:346
  103.8 1.7 %copy.9 = bf16[32,4096]{1,0:T(8,128)(2,1)} copy(bf16[32,4096]{1,0:T(8,128)(2,1)} %expert_layer.1) | data formatting | bytes 524288
